TPU v7x, 256 devices: a whole 4x4x8 slice. The times are simulated.
256 devices in a mesh: col: 8 (over z), row: 32 (over y, x, core).
Axes of the slice: x: 4, y: 4, z: 8, core: 2. Of those that a mesh axis runs over, the one named last changes fastest.
Arguments:
- matrix: bfloat16 [24576, 24576], P('row', 'col'), may hold values from -9 to 9
- left_basis: float32 [320, 24576], P(None, ('row', 'col')), may hold values from -6 to 6
- right_basis: float32 [320, 24576], P(None, ('col', 'row')), may hold values from -6 to 6
- right_block: float32 [64, 24576], P(None, ('col', 'row')), may hold values from -6 to 6
Outputs:
- left_blocks: float32 [64, 24576], P(None, ('row', 'col'))
- right_blocks: float32 [64, 24576], P(None, ('col', 'row'))
- factors: float32 [2, 64, 64], replicated
All inputs are finite; a program needn't handle non-finite values.
Results may differ from a plain program's by a relative error of at most 0.0041.
Values may be sent and summed in bfloat16 or wider, within the bound.
A program may use at most 64 MiB of HBM per device.

v0:
```python
import jax
import jax.numpy as jnp
from jax import lax
from jax.sharding import PartitionSpec as P

N = 24576


highest_precision = lax.Precision.HIGHEST


def contract(first, second, contracted):
    return lax.dot_general(first, second, (contracted, ((), ())), precision=highest_precision)


def summed(values):
    return lax.psum(values, ("col", "row"))


def orthonormalize(image, basis_set, basis_gram):
    coefficients = summed(contract(basis_set, image, ((1,), (1,)))) / N
    projected = image - contract(coefficients, basis_set, ((0,), (0,)))
    gram_matrix = summed(contract(projected, projected, ((1,), (1,)))) / N
    factor_low = jnp.linalg.cholesky(gram_matrix)
    new_block = lax.linalg.triangular_solve(factor_low, projected, left_side=True, lower=True)
    return (new_block, factor_low, basis_gram)


def forward(current, matrix):
    partial_sum = lax.dot_general(
        lax.all_gather(current, "row", axis=1, tiled=True),
        matrix,
        (((1,), (1,)), ((), ())),
        preferred_element_type=jnp.float32,
    )
    return lax.psum_scatter(partial_sum, "col", scatter_dimension=1, tiled=True)


def backward(left_new, matrix):
    partial_sum = jnp.dot(
        lax.all_gather(left_new, "col", axis=1, tiled=True),
        matrix,
        preferred_element_type=jnp.float32,
    )
    return lax.psum_scatter(partial_sum, "row", scatter_dimension=1, tiled=True)


def shards(matrix, left_basis, right_basis, right_block):
    right_set = jnp.concatenate([right_basis, right_block], 0)
    left_gram = None
    right_gram = None
    factor_list = []
    image = forward(right_block.astype(jnp.bfloat16), matrix)
    left_new, left_low, left_gram = orthonormalize(image, left_basis, left_gram)
    coimage = backward(left_new.astype(jnp.bfloat16), matrix)
    right_new, right_low, right_gram = orthonormalize(coimage, right_set, right_gram)
    factor_list.append(left_low)
    factor_list.append(right_low)
    return (left_new, right_new, jnp.stack(factor_list))


def solution(mesh):
    in_specs = (
        P("row", "col"),
        P(None, ("row", "col")),
        P(None, ("col", "row")),
        P(None, ("col", "row")),
    )
    out_specs = (P(None, ("row", "col")), P(None, ("col", "row")), P())
    return jax.shard_map(shards, mesh=mesh, in_specs=in_specs, out_specs=out_specs, check_vma=False)
```

profile of v0, /device:TPU:1, one launch (start us, length us, event | category | flops | bytes accessed | tf_op | source)
XLA Modules:
  0.0 866.0 jit_solution(16227857185204970658)
XLA Ops:
  7.2 0.0 copy-start
  7.2 0.0 reduce-scatter.7.cloned.1.call-start
  7.2 0.8 convert_bitcast_fusion.1
  8.0 26.4 %all-gather = bf16[32,96,64]{1,2,0:T(8,128)(2,1)S(1)} all-gather(bf16[1,96,64]{1,2,0:T(8,128)(2,1)S(1)} %convert_bitcast_fusion.1), channel_id=1, replica_groups=mesh['col'=8,'row'=32] {'row'}, dimensions={0}, use_global_device_ids=true | all-gather | bytes 405504 | tf_op jit(solution)/shard_map/all_gather | solution.py:31
  34.4 0.3 copy.19
  34.8 0.7 reshape.20
  35.5 4.4 convolution_bitcast_fusion.1
  39.9 0.0 reduce-scatter.7.cloned.1.call-update
  40.0 0.0 all-reduce.3.cloned.1.call-start
  40.0 32.8 %reduce-scatter.7.cloned.1.call-done = f32[96,64]{1,0:T(8,128)} async-done(((f32[768,64]{1,0:T(8,128)}), f32[96,64]{1,0:T(8,128)}) %reduce-scatter.7.cloned.1.call-update) | async-done | bytes 24592
  72.8 0.0 copy-done
  72.8 1.7 convolution_bitcast_fusion.2
  74.5 0.0 all-reduce.3.cloned.1.call-update
  74.6 0.0 reduce-scatter.9.cloned.1.call-start
  74.6 0.9 copy.29
  75.5 248.0 %all-reduce.3.cloned.1.call-done = f32[320,64]{0,1:T(8,128)} async-done(((f32[320,64]{0,1:T(8,128)}), f32[320,64]{0,1:T(8,128)}) %all-reduce.3.cloned.1.call-update) | async-done | bytes 81936 | tf_op jit(solution)/shard_map/psum | solution.py:17
  323.5 1.2 convolution_subtract_fusion.1
  324.7 0.0 copy-start.3
  324.7 0.0 copy-start.1
  324.7 0.2 fusion.20
  324.9 74.3 %psum.29 = f32[64,64]{0,1:T(8,128)S(1)} all-reduce(f32[64,64]{0,1:T(8,128)S(1)} %fusion.20), channel_id=1, replica_groups=mesh['col'=8,'row'=32] {'col','row'}, use_global_device_ids=true, to_apply=%region_2.0 | all-reduce | flops 4096 | bytes 32768 | tf_op jit(solution)/shard_map/psum | solution.py:17
  399.2 0.1 copy.21
  399.3 5.8 cholesky.44
  405.2 0.6 compare_reduce_fusion.1
  405.8 0.7 fusion.12
  406.5 4.9 custom-call.6
  411.4 0.3 fusion.8
  411.6 0.0 copy-start.2
  411.7 18.2 %all-gather.1 = bf16[8,96,64]{1,2,0:T(8,128)(2,1)S(1)} all-gather(bf16[1,96,64]{1,2,0:T(8,128)(2,1)S(1)} %convert_bitcast_fusion), channel_id=1, replica_groups=mesh['col'=8,'row'=32] {'col'}, dimensions={0}, use_global_device_ids=true | all-gather | bytes 110592 | tf_op jit(solution)/shard_map/all_gather | solution.py:41
  429.9 0.1 copy.22
  430.0 0.1 reshape.22
  430.1 5.4 convolution_bitcast_fusion
  435.5 0.0 reduce-scatter.9.cloned.1.call-update
  435.6 0.0 all-reduce.5.cloned.1.call-start
  435.6 0.0 copy-done.3
  435.6 0.1 copy.23
  435.7 85.8 %reduce-scatter.9.cloned.1.call-done = f32[96,64]{1,0:T(8,128)} async-done(((f32[3072,64]{1,0:T(8,128)}), f32[96,64]{1,0:T(8,128)}) %reduce-scatter.9.cloned.1.call-update) | async-done | bytes 24592
  521.6 0.0 copy-done.1
  521.6 1.7 fusion.2
  523.3 0.0 all-reduce.5.cloned.1.call-update
  523.3 0.9 copy.31
  524.2 245.7 %all-reduce.5.cloned.1.call-done = f32[384,64]{0,1:T(8,128)} async-done(((f32[384,64]{0,1:T(8,128)}), f32[384,64]{0,1:T(8,128)}) %all-reduce.5.cloned.1.call-update) | async-done | bytes 98320 | tf_op jit(solution)/shard_map/psum | solution.py:17
  769.9 1.2 convolution_subtract_fusion
  771.1 0.0 copy-done.2
  771.1 0.2 fusion.21
  771.3 74.5 %psum.31 = f32[64,64]{0,1:T(8,128)S(1)} all-reduce(f32[64,64]{0,1:T(8,128)S(1)} %fusion.21), channel_id=1, replica_groups=mesh['col'=8,'row'=32] {'col','row'}, use_global_device_ids=true, to_apply=%region_7.10 | all-reduce | flops 4096 | bytes 32768 | tf_op jit(solution)/shard_map/psum | solution.py:17
  845.8 0.1 copy.25
  845.9 5.8 cholesky.55
  851.8 0.6 compare_reduce_fusion
  852.4 0.7 fusion.13
  853.1 4.9 custom-call.7
  858.0 0.9 fusion.5
  858.8 0.6 pad_maximum_fusion.3
  (7 shorter events, 0.1 us)
Async XLA Ops:
  7.2 65.7 %copy-start = (f32[320,96]{0,1:T(8,128)S(1)}, f32[320,96]{0,1:T(8,128)}, u32[]{:S(2)}) copy-start(f32[320,96]{0,1:T(8,128)} %param.8) | copy-start | bytes 368644
  7.2 65.6 %reduce-scatter.7.cloned.1.call-start = ((), (), s32[]{:S(2)}) async-start(), calls=%async_computation.4 | async-start | bytes 442368
  40.0 283.5 %all-reduce.3.cloned.1.call-start = ((), (), s32[]{:S(2)}) async-start(), calls=%async_computation.2 | async-start | bytes 196608 | tf_op jit(solution)/shard_map/psum | solution.py:17
  74.6 447.0 %reduce-scatter.9.cloned.1.call-start = ((), (), s32[]{:S(2)}) async-start(), calls=%async_computation.5 | async-start | bytes 1622016
  324.7 110.9 %copy-start.3 = (f32[64,96]{1,0:T(8,128)S(1)}, f32[64,96]{1,0:T(8,128)}, u32[]{:S(2)}) copy-start(f32[64,96]{1,0:T(8,128)} %param.10) | copy-start | bytes 73732
  324.7 196.9 %copy-start.1 = (f32[320,96]{0,1:T(8,128)S(1)}, f32[320,96]{0,1:T(8,128)}, u32[]{:S(2)}) copy-start(f32[320,96]{0,1:T(8,128)} %param.9) | copy-start | bytes 368644
  411.6 359.5 %copy-start.2 = (f32[64,96]{1,0:T(8,128)}, f32[64,96]{1,0:T(8,128)S(1)}, u32[]{:S(2)}) copy-start(f32[64,96]{1,0:T(8,128)S(1)} %fusion.8) | copy-start | bytes 73732
  435.6 334.3 %all-reduce.5.cloned.1.call-start = ((), (), s32[]{:S(2)}) async-start(), calls=%async_computation.3 | async-start | bytes 196608 | tf_op jit(solution)/shard_map/psum | solution.py:17
Sparse Core Ops, SparseCore 0:
  40.1 32.6 reduce-scatter.6
  79.2 244.2 all-reduce.2
  435.7 85.8 reduce-scatter.8
  527.8 241.9 all-reduce.4
where the time goes:
time: 867 us; the launch traced here: 866 us
  waiting for transfers between devices  612 us (71%)
  blocking collectives  193 us (22%)
  other arithmetic  25.6 us (3%)
  matrix products  17.3 us (2%)
  between operations  13.9 us (2%)
    psum x2, waiting for transfers between devices, summed(): return lax.psum(values, ('col', 'row'))  494 us
    psum x2, blocking collectives, summed(): return lax.psum(values, ('col', 'row'))  149 us
    unnamed x6, waiting for transfers between devices  119 us
    all_gather x1, blocking collectives, forward(): lax.all_gather(current, 'row', axis=1, tiled=True)  26.4 us
    all_gather x1, blocking collectives, backward(): lax.all_gather(left_new, 'col', axis=1, tiled=True)  18.2 us
  transfers between devices with their start and end apart: 4, of which 4 were waited for; matrix products, arithmetic and copies ran while one was open for 0% of the time, Pallas kernels for 0%

commit v1 on v0

v1 whole, which is shorter than its diff:
```python
import jax
import jax.numpy as jnp
from jax import lax
from jax.experimental import pallas as pl
from jax.experimental.pallas import tpu as pltpu
from jax.sharding import PartitionSpec as P

N = 24576
BLOCK = 64
PRIOR_ROWS = 320
SET_ROWS = 384
COLS = 8
ROWS = 32
WIDTH = 96
LANES = 128
MESH = pl.DeviceIdType.MESH
F32 = jnp.float32
BF16 = jnp.bfloat16
highest_precision = lax.Precision.HIGHEST


def dot_nn(first, second):
    return lax.dot_general(first, second, (((1,), (0,)), ((), ())), precision=highest_precision, preferred_element_type=F32)


def dot_nt(first, second):
    return lax.dot_general(first, second, (((1,), (1,)), ((), ())), precision=highest_precision, preferred_element_type=F32)


def wait_bytes(ref, sem):
    pltpu.make_async_copy(ref, ref, sem).wait()


def lanes_of(shape):
    return lax.broadcasted_iota(jnp.int32, shape, 1)


def cholesky_and_inverse(gram):
    lane = lanes_of((8, LANES))
    sub = lax.broadcasted_iota(jnp.int32, (8, LANES), 0)
    blocks = []
    for k in range(8):
        unit = jnp.where(lane == sub + (BLOCK + 8 * k), 1.0, 0.0)
        padded = jnp.concatenate([gram[8 * k : 8 * k + 8, :], jnp.zeros((8, BLOCK), F32)], axis=1)
        blocks.append(padded + unit)
    for j in range(BLOCK):
        own, s = j // 8, j % 8
        row = blocks[own][s : s + 1, :]
        inv = lax.rsqrt(row[:, j : j + 1])
        scaled = row * inv
        for k in range(own, 8):
            factor = blocks[k][:, j : j + 1] * inv
            updated = blocks[k] - factor * scaled
            if k == own:
                updated = jnp.where(sub > s, updated, jnp.where(sub == s, jnp.broadcast_to(scaled, (8, LANES)), blocks[k]))
            blocks[k] = updated
    return jnp.concatenate(blocks, axis=0)


def kernel(
    matrix_hbm, left_hbm, right_hbm, block_hbm,
    left_out, right_out, factors_out,
    matrix, left_in, right_in, block_in,
    left_set, right_set,
    b_slots, b_all, image_send, image_recv,
    u_slots, u_all, co_send, co_recv,
    p_local, p_rs, p_ar, p_all,
    g_local, g_rs, g_ar, g_all,
    load_sem, send_sem, b_sem, image_sem, u_sem, co_sem,
    p_rs_sem, p_ar_sem, p_ag_sem, g_rs_sem, g_ar_sem, g_ag_sem,
):
    col = lax.axis_index("col")
    row = lax.axis_index("row")
    q_left = lax.rem(col, 4)
    q_right = lax.rem(row, 4)

    def row_peer(o):
        return lax.rem(row + o, ROWS)

    def col_peer(o):
        return lax.rem(col + o, COLS)

    barrier = pltpu.get_barrier_semaphore()

    def greet_row(o, carry):
        pl.semaphore_signal(barrier, inc=1, device_id=(col, row_peer(o)), device_id_type=MESH)
        return carry

    def greet_col(o, carry):
        pl.semaphore_signal(barrier, inc=1, device_id=(col_peer(o), row), device_id_type=MESH)
        return carry

    load_block = pltpu.make_async_copy(block_hbm, block_in, load_sem.at[0])
    load_left = pltpu.make_async_copy(left_hbm, left_in, load_sem.at[1])
    load_right = pltpu.make_async_copy(right_hbm, right_in, load_sem.at[2])
    load_matrix = pltpu.make_async_copy(matrix_hbm, matrix, load_sem.at[3])
    load_block.start()
    lax.fori_loop(1, ROWS, greet_row, 0)
    lax.fori_loop(1, COLS, greet_col, 0)
    load_left.start()
    load_right.start()
    load_matrix.start()

    def send_row(source, target, sem, send):
        def body(o, carry):
            peer = row_peer(o)
            pltpu.make_async_remote_copy(
                src_ref=source(o, peer), dst_ref=target(o), send_sem=send, recv_sem=sem,
                device_id=(col, peer), device_id_type=MESH,
            ).start()
            return carry

        lax.fori_loop(1, ROWS, body, 0)

    def send_col(source, target, sem, send):
        def body(o, carry):
            peer = col_peer(o)
            pltpu.make_async_remote_copy(
                src_ref=source(o, peer), dst_ref=target(o), send_sem=send, recv_sem=sem,
                device_id=(peer, row), device_id_type=MESH,
            ).start()
            return carry

        lax.fori_loop(1, COLS, body, 0)

    right_shift = lax.rem(96 * q_right, LANES)
    left_shift = lax.rem(96 * q_left, LANES)
    right_back = lax.rem(32 * q_right, LANES)
    left_back = lax.rem(32 * q_left, LANES)

    right_set[...] = jnp.zeros_like(right_set)
    left_set[...] = jnp.zeros_like(left_set)
    load_block.wait()
    right_set[PRIOR_ROWS:SET_ROWS, 0:WIDTH] = block_in[...]
    turned_block = pltpu.roll(right_set[PRIOR_ROWS:SET_ROWS, :], right_shift, 1)
    right_set[PRIOR_ROWS:SET_ROWS, :] = turned_block
    b_slots[row] = turned_block.astype(BF16)
    pl.semaphore_wait(barrier, ROWS + COLS - 2)
    send_row(lambda o, peer: b_slots.at[row], lambda o: b_slots.at[row], b_sem, send_sem.at[0])

    load_left.wait()
    left_set[0:PRIOR_ROWS, 0:WIDTH] = left_in[...]
    left_set[0:PRIOR_ROWS, :] = pltpu.roll(left_set[0:PRIOR_ROWS, :], left_shift, 1)
    load_right.wait()
    right_set[0:PRIOR_ROWS, 0:WIDTH] = right_in[...]
    right_set[0:PRIOR_ROWS, :] = pltpu.roll(right_set[0:PRIOR_ROWS, :], right_shift, 1)

    def start_gram(side, basis):
        k = 0
        for i in range(3):
            for j in range(i + 1):
                block = dot_nt(basis[128 * i : 128 * i + 128, :], basis[128 * j : 128 * j + 128, :])
                g_local[side, 128 * k : 128 * k + 128, :] = block
                k += 1

    def gram_rs_send(side):
        send_row(lambda o, peer: g_local.at[side, pl.ds(pl.multiple_of(24 * peer, 8), 24)], lambda o: g_rs.at[side, o - 1], g_rs_sem.at[side], send_sem.at[1 + side])

    def gram_ar_send(side):
        wait_bytes(g_rs.at[side], g_rs_sem.at[side])
        total = g_local[side, pl.ds(pl.multiple_of(24 * row, 8), 24), :]
        for o in range(ROWS - 1):
            total = total + g_rs[side, o]
        g_ar[side, col] = total
        send_col(lambda o, peer: g_ar.at[side, col], lambda o: g_ar.at[side, col], g_ar_sem.at[side], send_sem.at[3 + side])

    def gram_ag_send(side):
        wait_bytes(g_ar.at[side, pl.ds(0, COLS - 1)], g_ar_sem.at[side])
        total = g_ar[side, 0]
        for c in range(1, COLS):
            total = total + g_ar[side, c]
        g_all[side, row] = total
        send_row(lambda o, peer: g_all.at[side, row], lambda o: g_all.at[side, row], g_ag_sem.at[side], send_sem.at[5 + side])

    def gram_wait(side):
        wait_bytes(g_all.at[side, pl.ds(0, ROWS - 1)], g_ag_sem.at[side])

    start_gram(0, left_set)

    lane16 = lanes_of((BLOCK, LANES))

    def joined(slots, out, count):
        for group in range(count // 4):
            first, second, third, fourth = (slots[4 * group + k].astype(F32) for k in range(4))
            base = 3 * LANES * group
            out[:, base : base + 128] = jnp.where(lane16 < 96, first, second).astype(BF16)
            out[:, base + 128 : base + 256] = jnp.where(lane16 < 64, second, third).astype(BF16)
            out[:, base + 256 : base + 384] = jnp.where(lane16 < 32, third, fourth).astype(BF16)

    def pieces(values):
        first, second, third = (values[:, 128 * k : 128 * k + 128] for k in range(3))
        return (first, jnp.where(lane16 < 64, second, first), jnp.where(lane16 < 64, third, second), third)

    wait_bytes(b_slots.at[pl.ds(0, ROWS - 1)], b_sem)
    gram_rs_send(0)
    joined(b_slots, b_all, ROWS)
    load_matrix.wait()
    for half in range(2):
        part = lax.dot_general(
            b_all[...], matrix[384 * half : 384 * half + 384, :], (((1,), (1,)), ((), ())), preferred_element_type=F32
        )
        for k, piece in enumerate(pieces(part)):
            image_send[4 * half + k] = piece
    send_col(lambda o, peer: image_send.at[peer], lambda o: image_recv.at[o - 1], image_sem, send_sem.at[7])
    start_gram(1, right_set)
    wait_bytes(image_recv, image_sem)
    valid_left = lax.rem(lane16 + 32 * q_left, LANES) < WIDTH
    valid_right = lax.rem(lane16 + 32 * q_right, LANES) < WIDTH
    image = image_send[col]
    for o in range(COLS - 1):
        image = image + image_recv[o]
    image = jnp.where(valid_left, image, 0.0)

    def sums_rs_send(side, values, basis):
        for i in range(3):
            p_local[side, 64 * i : 64 * i + 64, :] = dot_nt(values, basis[128 * i : 128 * i + 128, :])
        p_local[side, 192:256, 0:BLOCK] = dot_nt(values, values)
        p_local[side, 192:256, BLOCK:LANES] = jnp.zeros((BLOCK, LANES - BLOCK), F32)
        send_row(lambda o, peer: p_local.at[side, pl.ds(pl.multiple_of(8 * peer, 8), 8)], lambda o: p_rs.at[side, o - 1], p_rs_sem.at[side], send_sem.at[8 + side])

    def sums_ar_send(side):
        wait_bytes(p_rs.at[side], p_rs_sem.at[side])
        total = p_local[side, pl.ds(pl.multiple_of(8 * row, 8), 8), :]
        for o in range(ROWS - 1):
            total = total + p_rs[side, o]
        p_ar[side, col] = total
        send_col(lambda o, peer: p_ar.at[side, col], lambda o: p_ar.at[side, col], p_ar_sem.at[side], send_sem.at[10 + side])

    def sums_ag_send(side):
        wait_bytes(p_ar.at[side, pl.ds(0, COLS - 1)], p_ar_sem.at[side])
        total = p_ar[side, 0]
        for c in range(1, COLS):
            total = total + p_ar[side, c]
        p_all[side, row] = total
        send_row(lambda o, peer: p_all.at[side, row], lambda o: p_all.at[side, row], p_ag_sem.at[side], send_sem.at[12 + side])

    def sums_wait(side):
        wait_bytes(p_all.at[side, pl.ds(0, ROWS - 1)], p_ag_sem.at[side])

    def finish(side, values, basis):
        sums = [jnp.concatenate([p_all[side, 8 * i + t] for t in range(8)], axis=0) for i in range(4)]
        coefficients = [sums[i] * (1.0 / N) for i in range(3)]
        gram_blocks = {}
        k = 0
        for i in range(3):
            for j in range(i + 1):
                gram_blocks[(i, j)] = jnp.concatenate([g_all[side, (128 * k + 8 * t) // 24, (128 * k + 8 * t) % 24 : (128 * k + 8 * t) % 24 + 8, :] for t in range(16)], axis=0)
                k += 1
        gram = sums[3][:, 0:BLOCK]
        for j in range(3):
            along = 2.0 * sums[j]
            for i in range(3):
                if i >= j:
                    along = along - dot_nn(coefficients[i], gram_blocks[(i, j)])
                else:
                    along = along - dot_nt(coefficients[i], gram_blocks[(j, i)])
            gram = gram - dot_nt(along, coefficients[j])
        projected = values
        for i in range(3):
            projected = projected - dot_nn(coefficients[i], basis[128 * i : 128 * i + 128, :])
        eliminated = cholesky_and_inverse(gram * (1.0 / N))
        new_block = dot_nn(eliminated[:, BLOCK:LANES], projected)
        upper = jnp.where(lane16 >= lax.broadcasted_iota(jnp.int32, (BLOCK, LANES), 0), eliminated, 0.0)
        return new_block, upper

    def write_factor(side, upper):
        factors_out[side] = jnp.transpose(upper)[0:BLOCK, :]

    sums_rs_send(0, image, left_set)
    gram_ar_send(0)
    sums_ar_send(0)
    gram_ag_send(0)
    sums_ag_send(0)
    gram_wait(0)
    sums_wait(0)
    gram_rs_send(1)
    left_new, left_upper = finish(0, image, left_set)
    u_slots[col] = left_new.astype(BF16)
    send_col(lambda o, peer: u_slots.at[col], lambda o: u_slots.at[col], u_sem, send_sem.at[14])
    gram_ar_send(1)
    left_out[...] = pltpu.roll(left_new, left_back, 1)[:, 0:WIDTH]
    write_factor(0, left_upper)

    wait_bytes(u_slots.at[pl.ds(0, COLS - 1)], u_sem)
    joined(u_slots, u_all, COLS)
    for group in range(8):
        part = lax.dot_general(
            u_all[...], matrix[:, 384 * group : 384 * group + 384], (((1,), (0,)), ((), ())), preferred_element_type=F32
        )
        for k, piece in enumerate(pieces(part)):
            co_send[4 * group + k] = piece.astype(BF16)
    send_row(lambda o, peer: co_send.at[peer], lambda o: co_recv.at[o - 1], co_sem, send_sem.at[15])
    wait_bytes(co_recv, co_sem)
    coimage = co_send[row].astype(F32)
    for o in range(ROWS - 1):
        coimage = coimage + co_recv[o].astype(F32)
    coimage = jnp.where(valid_right, coimage, 0.0)
    sums_rs_send(1, coimage, right_set)
    sums_ar_send(1)
    gram_ag_send(1)
    sums_ag_send(1)
    gram_wait(1)
    sums_wait(1)
    right_new, right_upper = finish(1, coimage, right_set)
    right_out[...] = pltpu.roll(right_new, right_back, 1)[:, 0:WIDTH]
    write_factor(1, right_upper)

    wait_bytes(b_slots.at[pl.ds(0, ROWS - 1)], send_sem.at[0])
    wait_bytes(image_recv, send_sem.at[7])
    wait_bytes(u_slots.at[pl.ds(0, COLS - 1)], send_sem.at[14])
    wait_bytes(co_recv, send_sem.at[15])
    for side in range(2):
        wait_bytes(g_rs.at[side], send_sem.at[1 + side])
        wait_bytes(g_ar.at[side, pl.ds(0, COLS - 1)], send_sem.at[3 + side])
        wait_bytes(g_all.at[side, pl.ds(0, ROWS - 1)], send_sem.at[5 + side])
        wait_bytes(p_rs.at[side], send_sem.at[8 + side])
        wait_bytes(p_ar.at[side, pl.ds(0, COLS - 1)], send_sem.at[10 + side])
        wait_bytes(p_all.at[side, pl.ds(0, ROWS - 1)], send_sem.at[12 + side])


def shards(matrix, left_basis, right_basis, right_block):
    any_space = pl.BlockSpec(memory_space=pl.ANY)
    in_vmem = pl.BlockSpec(memory_space=pltpu.VMEM)
    dma = pltpu.SemaphoreType.DMA
    return pl.pallas_call(
        kernel,
        out_shape=(
            jax.ShapeDtypeStruct((BLOCK, WIDTH), F32),
            jax.ShapeDtypeStruct((BLOCK, WIDTH), F32),
            jax.ShapeDtypeStruct((2, BLOCK, BLOCK), F32),
        ),
        in_specs=[any_space] * 4,
        out_specs=(in_vmem, in_vmem, in_vmem),
        scratch_shapes=[
            pltpu.VMEM((768, 3072), BF16),
            pltpu.VMEM((PRIOR_ROWS, WIDTH), F32),
            pltpu.VMEM((PRIOR_ROWS, WIDTH), F32),
            pltpu.VMEM((BLOCK, WIDTH), F32),
            pltpu.VMEM((SET_ROWS, LANES), F32),
            pltpu.VMEM((SET_ROWS, LANES), F32),
            pltpu.VMEM((ROWS, BLOCK, LANES), BF16),
            pltpu.VMEM((BLOCK, 3072), BF16),
            pltpu.VMEM((COLS, BLOCK, LANES), F32),
            pltpu.VMEM((COLS - 1, BLOCK, LANES), F32),
            pltpu.VMEM((COLS, BLOCK, LANES), BF16),
            pltpu.VMEM((BLOCK, 768), BF16),
            pltpu.VMEM((ROWS, BLOCK, LANES), BF16),
            pltpu.VMEM((ROWS - 1, BLOCK, LANES), BF16),
            pltpu.VMEM((2, 256, LANES), F32),
            pltpu.VMEM((2, ROWS - 1, 8, LANES), F32),
            pltpu.VMEM((2, COLS, 8, LANES), F32),
            pltpu.VMEM((2, ROWS, 8, LANES), F32),
            pltpu.VMEM((2, 768, LANES), F32),
            pltpu.VMEM((2, ROWS - 1, 24, LANES), F32),
            pltpu.VMEM((2, COLS, 24, LANES), F32),
            pltpu.VMEM((2, ROWS, 24, LANES), F32),
            dma((4,)), dma((16,)), dma(()), dma(()), dma(()), dma(()),
            dma((2,)), dma((2,)), dma((2,)), dma((2,)), dma((2,)), dma((2,)),
        ],
        compiler_params=pltpu.CompilerParams(
            collective_id=0, has_side_effects=True, vmem_limit_bytes=48 * 1024 * 1024
        ),
        cost_estimate=pl.CostEstimate(flops=700_000_000, bytes_accessed=8_000_000, transcendentals=0),
    )(matrix, left_basis, right_basis, right_block)


def solution(mesh):
    in_specs = (
        P("row", "col"),
        P(None, ("row", "col")),
        P(None, ("col", "row")),
        P(None, ("col", "row")),
    )
    out_specs = (P(None, ("row", "col")), P(None, ("col", "row")), P())
    return jax.shard_map(shards, mesh=mesh, in_specs=in_specs, out_specs=out_specs, check_vma=False)
```

time: 867 us -> 98.7 us (0.11)
  waiting for transfers between devices: 612 us -> 0 us
  blocking collectives: 193 us -> 0 us
  Pallas kernels: 0 us -> 90.8 us
  other arithmetic: 25.6 us -> 0 us
  matrix products: 17.3 us -> 0 us
  between operations: 13.9 us -> 0.65 us
    psum x2 -> x0, waiting for transfers between devices: 494 us -> none  [summed(): return lax.psum(values, ('col', 'row'))]
    psum x2 -> x0, blocking collectives: 149 us -> none  [summed(): return lax.psum(values, ('col', 'row'))]
    unnamed x6 -> x0, waiting for transfers between devices: 119 us -> none
    pallas_call x0 -> x1, Pallas kernels: none -> 90.8 us  [shards(): pl.pallas_call(kernel, out_shape=(jax.ShapeDtypeStruct((BLOCK, WIDTH), F3...]
    all_gather x2 -> x0, blocking collectives: 44.6 us -> none  [the longest x1 26.4 us: forward(): lax.all_gather(current, 'row', axis=1, tiled=True)]
    another operation x11 -> x0, other arithmetic: 24.8 us -> none  [the longest x6 13 us: orthonormalize(): factor_low = jnp.linalg.cholesky(gram_matrix)]
    unnamed x2 -> x0, matrix products: 9.88 us -> none
  transfers between devices with their start and end apart: 4 -> 0, of which waited for: 4 -> 0; matrix products, arithmetic and copies ran while one was open for 0% -> 0% of each run, Pallas kernels for 0% -> 0%
where the time goes in v1:
time: 98.7 us; the launch traced here: 98.4 us
  Pallas kernels  90.8 us (92%)
  local copies, waits for them, and re-layouts  7 us (7%)
    pallas_call x1, Pallas kernels, shards(): pl.pallas_call(kernel, out_shape=(jax.ShapeDtypeStruct((BLOCK, WIDTH), F3...  90.8 us
    unnamed x9, local copies, waits for them, and re-layouts  7 us

profile of v1, /device:TPU:1, one launch (start us, length us, event | category | flops | bytes accessed | tf_op | source)
XLA Modules:
  0.0 98.4 jit_solution(12442061009680571903)
XLA Ops:
  0.6 1.0 %copy.7.left_hbm = f32[320,96]{1,0:T(8,128)S(1)} copy(f32[320,96]{0,1:T(8,128)} %param.5) | data formatting | bytes 245760 | tf_op args[1]
  1.7 1.0 %copy.8.right_hbm = f32[320,96]{1,0:T(8,128)S(1)} copy(f32[320,96]{0,1:T(8,128)} %param.6) | data formatting | bytes 245760 | tf_op args[2]
  2.7 0.0 copy-start
  2.7 2.3 %copy-done = bf16[768,3072]{1,0:T(8,128)(2,1)S(1)} copy-done((bf16[768,3072]{1,0:T(8,128)(2,1)S(1)}, bf16[768,3072]{1,0:T(8,128)(2,1)}, u32[]{:S(2)}) %copy-start) | copy-done | bytes 4718616
  5.0 0.0 copy-start.1
  5.0 0.8 copy-done.1
  5.8 90.8 %shard_map.67 = (f32[64,96]{1,0:T(8,128)S(1)}, f32[64,96]{1,0:T(8,128)S(1)}, f32[2,64,64]{2,1,0:T(8,128)S(1)}) custom-call(bf16[768,3072]{1,0:T(8,128)(2,1)S(1)} %copy-done, f32[320,96]{1,0:T(8,128)S(1)} %copy.7.left_hbm, f32[320,96]{1,0:T(8,128)S(1)} %copy.8.right_hbm, f32[64,96]{1,0:T(8,128)S(1)} %copy-done.1), custom_call_target="tpu_custom_call" | custom-call | flops 700000000 | bytes 8000000 | tf_op jit(solution)/shard_map/pallas_call | solution.py:325
  96.6 0.6 copy.12
  97.2 0.6 copy.13
  97.8 0.6 copy.14
Async XLA Ops:
  2.7 2.3 %copy-start = (bf16[768,3072]{1,0:T(8,128)(2,1)S(1)}, bf16[768,3072]{1,0:T(8,128)(2,1)}, u32[]{:S(2)}) copy-start(bf16[768,3072]{1,0:T(8,128)(2,1)} %matrix_hbm.1) | copy-start | bytes 14155780
  5.0 0.8 copy-start.1

commit v2 on v1

--- a/solution.py
+++ b/solution.py
@@ -38,22 +38,28 @@
 def cholesky_and_inverse(gram):
     lane = lanes_of((8, LANES))
     sub = lax.broadcasted_iota(jnp.int32, (8, LANES), 0)
+
+    def spread(values):
+        return jnp.broadcast_to(values, (8, LANES))
+
     blocks = []
     for k in range(8):
         unit = jnp.where(lane == sub + (BLOCK + 8 * k), 1.0, 0.0)
         padded = jnp.concatenate([gram[8 * k : 8 * k + 8, :], jnp.zeros((8, BLOCK), F32)], axis=1)
         blocks.append(padded + unit)
-    for j in range(BLOCK):
-        own, s = j // 8, j % 8
-        row = blocks[own][s : s + 1, :]
-        inv = lax.rsqrt(row[:, j : j + 1])
-        scaled = row * inv
-        for k in range(own, 8):
-            factor = blocks[k][:, j : j + 1] * inv
-            updated = blocks[k] - factor * scaled
-            if k == own:
-                updated = jnp.where(sub > s, updated, jnp.where(sub == s, jnp.broadcast_to(scaled, (8, LANES)), blocks[k]))
-            blocks[k] = updated
+    for b in range(8):
+        columns = [[spread(blocks[k][:, 8 * b + i : 8 * b + i + 1]) for k in range(b, 8)] for i in range(8)]
+        for i in range(8):
+            inverse = lax.rsqrt(spread(columns[i][0][i : i + 1, :]))
+            lower = [column * inverse for column in columns[i]]
+            row = spread(blocks[b][i : i + 1, :]) * inverse
+            for m in range(i + 1, 8):
+                weight = spread(lower[0][m : m + 1, :])
+                columns[m] = [column - below * weight for column, below in zip(columns[m], lower)]
+            updated = blocks[b] - lower[0] * row
+            blocks[b] = jnp.where(sub > i, updated, jnp.where(sub == i, row, blocks[b]))
+            for k in range(b + 1, 8):
+                blocks[k] = blocks[k] - lower[k - b] * row
     return jnp.concatenate(blocks, axis=0)
 
 
@@ -61,11 +67,11 @@
     matrix_hbm, left_hbm, right_hbm, block_hbm,
     left_out, right_out, factors_out,
     matrix, left_in, right_in, block_in,
-    left_set, right_set,
-    b_slots, b_all, image_send, image_recv,
+    turned, left_set, right_set,
+    b_slots, b_all, image_sum, image_send, image_recv,
     u_slots, u_all, co_send, co_recv,
     p_local, p_rs, p_ar, p_all,
-    g_local, g_rs, g_ar, g_all,
+    g_local, g_rs, g_ar, g_all, weights,
     load_sem, send_sem, b_sem, image_sem, u_sem, co_sem,
     p_rs_sem, p_ar_sem, p_ag_sem, g_rs_sem, g_ar_sem, g_ag_sem,
 ):
@@ -102,7 +108,8 @@
     load_matrix.start()
 
     def send_row(source, target, sem, send):
-        def body(o, carry):
+        def body(k, carry):
+            o = lax.rem(k + 15, ROWS - 1) + 1
             peer = row_peer(o)
             pltpu.make_async_remote_copy(
                 src_ref=source(o, peer), dst_ref=target(o), send_sem=send, recv_sem=sem,
@@ -110,10 +117,11 @@
             ).start()
             return carry
 
-        lax.fori_loop(1, ROWS, body, 0)
+        lax.fori_loop(0, ROWS - 1, body, 0)
 
     def send_col(source, target, sem, send):
-        def body(o, carry):
+        def body(k, carry):
+            o = lax.rem(k + 3, COLS - 1) + 1
             peer = col_peer(o)
             pltpu.make_async_remote_copy(
                 src_ref=source(o, peer), dst_ref=target(o), send_sem=send, recv_sem=sem,
@@ -121,29 +129,58 @@
             ).start()
             return carry
 
-        lax.fori_loop(1, COLS, body, 0)
+        lax.fori_loop(0, COLS - 1, body, 0)
 
     right_shift = lax.rem(96 * q_right, LANES)
-    left_shift = lax.rem(96 * q_left, LANES)
     right_back = lax.rem(32 * q_right, LANES)
     left_back = lax.rem(32 * q_left, LANES)
 
-    right_set[...] = jnp.zeros_like(right_set)
-    left_set[...] = jnp.zeros_like(left_set)
+    turned[...] = jnp.zeros_like(turned)
     load_block.wait()
-    right_set[PRIOR_ROWS:SET_ROWS, 0:WIDTH] = block_in[...]
-    turned_block = pltpu.roll(right_set[PRIOR_ROWS:SET_ROWS, :], right_shift, 1)
-    right_set[PRIOR_ROWS:SET_ROWS, :] = turned_block
+    left_set[0:BLOCK, :] = jnp.zeros((BLOCK, LANES), F32)
+    left_set[0:BLOCK, 0:WIDTH] = block_in[...]
+    turned_block = pltpu.roll(left_set[0:BLOCK, :], right_shift, 1)
     b_slots[row] = turned_block.astype(BF16)
     pl.semaphore_wait(barrier, ROWS + COLS - 2)
-    send_row(lambda o, peer: b_slots.at[row], lambda o: b_slots.at[row], b_sem, send_sem.at[0])
+    plane, within = row // 8, lax.rem(row, 8)
+
+    def own_plane_peer(w):
+        return plane * 8 + lax.rem(within + w, 8)
+
+    def other_plane_peer(y, w):
+        return lax.rem(plane + y, 4) * 8 + lax.rem(within + w, 8)
+
+    def send_block(peer, y):
+        pltpu.make_async_remote_copy(
+            src_ref=b_slots.at[row], dst_ref=b_slots.at[row], send_sem=send_sem.at[0], recv_sem=b_sem.at[y],
+            device_id=(col, peer), device_id_type=MESH,
+        ).start()
+
+    def send_block_near(w, carry):
+        send_block(own_plane_peer(w), 0)
+        return carry
+
+    lax.fori_loop(1, 8, send_block_near, 0)
+    for y in (1, 3, 2):
+        def send_block_far(w, carry, y=y):
+            send_block(other_plane_peer(y, w), y)
+            return carry
+
+        lax.fori_loop(0, 8, send_block_far, 0)
+
+    def turn(basis, q, out):
+        for k in range(3):
+            place = pl.multiple_of(32 * lax.rem(k + 3 * q, 4), 32)
+            turned[pl.ds(place, 32), 0:PRIOR_ROWS] = basis[32 * k : 32 * k + 32, :]
+        turned[pl.ds(pl.multiple_of(32 * lax.rem(3 + 3 * q, 4), 32), 32), :] = jnp.zeros((32, SET_ROWS), F32)
+        for i in range(3):
+            out[128 * i : 128 * i + 128, :] = jnp.transpose(turned[:, 128 * i : 128 * i + 128])
 
     load_left.wait()
-    left_set[0:PRIOR_ROWS, 0:WIDTH] = left_in[...]
-    left_set[0:PRIOR_ROWS, :] = pltpu.roll(left_set[0:PRIOR_ROWS, :], left_shift, 1)
+    turn(left_in, q_left, left_set)
     load_right.wait()
-    right_set[0:PRIOR_ROWS, 0:WIDTH] = right_in[...]
-    right_set[0:PRIOR_ROWS, :] = pltpu.roll(right_set[0:PRIOR_ROWS, :], right_shift, 1)
+    turn(right_in, q_right, right_set)
+    right_set[PRIOR_ROWS:SET_ROWS, :] = turned_block
 
     def start_gram(side, basis):
         k = 0
@@ -174,32 +211,53 @@
 
     def gram_wait(side):
         wait_bytes(g_all.at[side, pl.ds(0, ROWS - 1)], g_ag_sem.at[side])
+        k = 0
+        for i in range(3):
+            for j in range(i + 1):
+                for t in range(16):
+                    at = 128 * k + 8 * t
+                    weights[128 * i + 8 * t : 128 * i + 8 * t + 8, 128 * j : 128 * j + 128] = g_all[side, at // 24, at % 24 : at % 24 + 8, :] * (-1.0 / N / N)
+                block = weights[128 * i : 128 * i + 128, 128 * j : 128 * j + 128]
+                if i == j:
+                    same = lanes_of((128, LANES)) == lax.broadcasted_iota(jnp.int32, (128, LANES), 0)
+                    weights[128 * i : 128 * i + 128, 128 * j : 128 * j + 128] = block + jnp.where(same, 2.0 / N, 0.0)
+                else:
+                    weights[128 * j : 128 * j + 128, 128 * i : 128 * i + 128] = jnp.transpose(block)
+                k += 1
 
     start_gram(0, left_set)
 
     lane16 = lanes_of((BLOCK, LANES))
 
-    def joined(slots, out, count):
-        for group in range(count // 4):
-            first, second, third, fourth = (slots[4 * group + k].astype(F32) for k in range(4))
-            base = 3 * LANES * group
-            out[:, base : base + 128] = jnp.where(lane16 < 96, first, second).astype(BF16)
-            out[:, base + 128 : base + 256] = jnp.where(lane16 < 64, second, third).astype(BF16)
-            out[:, base + 256 : base + 384] = jnp.where(lane16 < 32, third, fourth).astype(BF16)
+    def joined(slots):
+        chunks = []
+        for group in range(2):
+            first, second, third, fourth = (slots(4 * group + k).astype(F32) for k in range(4))
+            chunks.append(jnp.where(lane16 < 96, first, second).astype(BF16))
+            chunks.append(jnp.where(lane16 < 64, second, third).astype(BF16))
+            chunks.append(jnp.where(lane16 < 32, third, fourth).astype(BF16))
+        return jnp.concatenate(chunks, axis=1)
 
     def pieces(values):
         first, second, third = (values[:, 128 * k : 128 * k + 128] for k in range(3))
         return (first, jnp.where(lane16 < 64, second, first), jnp.where(lane16 < 64, third, second), third)
 
-    wait_bytes(b_slots.at[pl.ds(0, ROWS - 1)], b_sem)
-    gram_rs_send(0)
-    joined(b_slots, b_all, ROWS)
     load_matrix.wait()
+    for y in (0, 1, 3, 2):
+        wait_bytes(b_slots.at[pl.ds(0, 7 if y == 0 else 8)], b_sem.at[y])
+        source = lax.rem(plane + (4 - y), 4)
+        b_all[...] = joined(lambda k: b_slots[8 * source + k])
+        if y == 2:
+            gram_rs_send(0)
+        part = lax.dot_general(
+            b_all[...], matrix[:, pl.ds(pl.multiple_of(768 * source, 768), 768)], (((1,), (1,)), ((), ())), preferred_element_type=F32
+        )
+        if y == 0:
+            image_sum[...] = part
+        else:
+            image_sum[...] += part
     for half in range(2):
-        part = lax.dot_general(
-            b_all[...], matrix[384 * half : 384 * half + 384, :], (((1,), (1,)), ((), ())), preferred_element_type=F32
-        )
-        for k, piece in enumerate(pieces(part)):
+        for k, piece in enumerate(pieces(image_sum[:, 384 * half : 384 * half + 384])):
             image_send[4 * half + k] = piece
     send_col(lambda o, peer: image_send.at[peer], lambda o: image_recv.at[o - 1], image_sem, send_sem.at[7])
     start_gram(1, right_set)
@@ -239,25 +297,9 @@
 
     def finish(side, values, basis):
         sums = [jnp.concatenate([p_all[side, 8 * i + t] for t in range(8)], axis=0) for i in range(4)]
-        coefficients = [sums[i] * (1.0 / N) for i in range(3)]
-        gram_blocks = {}
-        k = 0
-        for i in range(3):
-            for j in range(i + 1):
-                gram_blocks[(i, j)] = jnp.concatenate([g_all[side, (128 * k + 8 * t) // 24, (128 * k + 8 * t) % 24 : (128 * k + 8 * t) % 24 + 8, :] for t in range(16)], axis=0)
-                k += 1
-        gram = sums[3][:, 0:BLOCK]
-        for j in range(3):
-            along = 2.0 * sums[j]
-            for i in range(3):
-                if i >= j:
-                    along = along - dot_nn(coefficients[i], gram_blocks[(i, j)])
-                else:
-                    along = along - dot_nt(coefficients[i], gram_blocks[(j, i)])
-            gram = gram - dot_nt(along, coefficients[j])
-        projected = values
-        for i in range(3):
-            projected = projected - dot_nn(coefficients[i], basis[128 * i : 128 * i + 128, :])
+        joint = jnp.concatenate(sums[0:3], axis=1)
+        gram = sums[3][:, 0:BLOCK] - dot_nt(dot_nn(joint, weights[...]), joint)
+        projected = values - dot_nn(joint * (1.0 / N), basis[...])
         eliminated = cholesky_and_inverse(gram * (1.0 / N))
         new_block = dot_nn(eliminated[:, BLOCK:LANES], projected)
         upper = jnp.where(lane16 >= lax.broadcasted_iota(jnp.int32, (BLOCK, LANES), 0), eliminated, 0.0)
@@ -282,18 +324,40 @@
     write_factor(0, left_upper)
 
     wait_bytes(u_slots.at[pl.ds(0, COLS - 1)], u_sem)
-    joined(u_slots, u_all, COLS)
-    for group in range(8):
+    u_all[...] = joined(lambda k: u_slots[k])
+
+    def send_piece(peer, y):
+        pltpu.make_async_remote_copy(
+            src_ref=co_send.at[peer], dst_ref=co_recv.at[8 * y + within], send_sem=send_sem.at[15], recv_sem=co_sem.at[y],
+            device_id=(col, peer), device_id_type=MESH,
+        ).start()
+
+    for y in (2, 1, 3, 0):
+        target = lax.rem(plane + y, 4)
         part = lax.dot_general(
-            u_all[...], matrix[:, 384 * group : 384 * group + 384], (((1,), (0,)), ((), ())), preferred_element_type=F32
+            u_all[...], matrix[:, pl.ds(pl.multiple_of(768 * target, 768), 768)], (((1,), (0,)), ((), ())), preferred_element_type=F32
         )
-        for k, piece in enumerate(pieces(part)):
-            co_send[4 * group + k] = piece.astype(BF16)
-    send_row(lambda o, peer: co_send.at[peer], lambda o: co_recv.at[o - 1], co_sem, send_sem.at[15])
-    wait_bytes(co_recv, co_sem)
-    coimage = co_send[row].astype(F32)
-    for o in range(ROWS - 1):
-        coimage = coimage + co_recv[o].astype(F32)
+        for half in range(2):
+            for k, piece in enumerate(pieces(part[:, 384 * half : 384 * half + 384])):
+                co_send[8 * target + 4 * half + k] = piece.astype(BF16)
+        if y == 0:
+            def send_piece_near(w, carry):
+                send_piece(own_plane_peer(w), 0)
+                return carry
+
+            lax.fori_loop(1, 8, send_piece_near, 0)
+        else:
+            def send_piece_far(w, carry, y=y):
+                send_piece(other_plane_peer(y, w), y)
+                return carry
+
+            lax.fori_loop(0, 8, send_piece_far, 0)
+    co_recv[within] = co_send[row]
+    coimage = jnp.zeros((BLOCK, LANES), F32)
+    for y in (0, 1, 3, 2):
+        wait_bytes(co_recv.at[pl.ds(8 * y, 7 if y == 0 else 8)], co_sem.at[y])
+        for w in range(8):
+            coimage = coimage + co_recv[8 * y + w].astype(F32)
     coimage = jnp.where(valid_right, coimage, 0.0)
     sums_rs_send(1, coimage, right_set)
     sums_ar_send(1)
@@ -308,7 +372,7 @@
     wait_bytes(b_slots.at[pl.ds(0, ROWS - 1)], send_sem.at[0])
     wait_bytes(image_recv, send_sem.at[7])
     wait_bytes(u_slots.at[pl.ds(0, COLS - 1)], send_sem.at[14])
-    wait_bytes(co_recv, send_sem.at[15])
+    wait_bytes(co_recv.at[pl.ds(0, ROWS - 1)], send_sem.at[15])
     for side in range(2):
         wait_bytes(g_rs.at[side], send_sem.at[1 + side])
         wait_bytes(g_ar.at[side, pl.ds(0, COLS - 1)], send_sem.at[3 + side])
@@ -319,7 +383,7 @@
 
 
 def shards(matrix, left_basis, right_basis, right_block):
-    any_space = pl.BlockSpec(memory_space=pl.ANY)
+    in_hbm = pl.BlockSpec(memory_space=pltpu.HBM)
     in_vmem = pl.BlockSpec(memory_space=pltpu.VMEM)
     dma = pltpu.SemaphoreType.DMA
     return pl.pallas_call(
@@ -329,23 +393,25 @@
             jax.ShapeDtypeStruct((BLOCK, WIDTH), F32),
             jax.ShapeDtypeStruct((2, BLOCK, BLOCK), F32),
         ),
-        in_specs=[any_space] * 4,
+        in_specs=[in_hbm] * 4,
         out_specs=(in_vmem, in_vmem, in_vmem),
         scratch_shapes=[
             pltpu.VMEM((768, 3072), BF16),
-            pltpu.VMEM((PRIOR_ROWS, WIDTH), F32),
-            pltpu.VMEM((PRIOR_ROWS, WIDTH), F32),
+            pltpu.VMEM((WIDTH, PRIOR_ROWS), F32),
+            pltpu.VMEM((WIDTH, PRIOR_ROWS), F32),
             pltpu.VMEM((BLOCK, WIDTH), F32),
+            pltpu.VMEM((LANES, SET_ROWS), F32),
             pltpu.VMEM((SET_ROWS, LANES), F32),
             pltpu.VMEM((SET_ROWS, LANES), F32),
             pltpu.VMEM((ROWS, BLOCK, LANES), BF16),
-            pltpu.VMEM((BLOCK, 3072), BF16),
+            pltpu.VMEM((BLOCK, 768), BF16),
+            pltpu.VMEM((BLOCK, 768), F32),
             pltpu.VMEM((COLS, BLOCK, LANES), F32),
             pltpu.VMEM((COLS - 1, BLOCK, LANES), F32),
             pltpu.VMEM((COLS, BLOCK, LANES), BF16),
             pltpu.VMEM((BLOCK, 768), BF16),
             pltpu.VMEM((ROWS, BLOCK, LANES), BF16),
-            pltpu.VMEM((ROWS - 1, BLOCK, LANES), BF16),
+            pltpu.VMEM((ROWS, BLOCK, LANES), BF16),
             pltpu.VMEM((2, 256, LANES), F32),
             pltpu.VMEM((2, ROWS - 1, 8, LANES), F32),
             pltpu.VMEM((2, COLS, 8, LANES), F32),
@@ -354,14 +420,15 @@
             pltpu.VMEM((2, ROWS - 1, 24, LANES), F32),
             pltpu.VMEM((2, COLS, 24, LANES), F32),
             pltpu.VMEM((2, ROWS, 24, LANES), F32),
-            dma((4,)), dma((16,)), dma(()), dma(()), dma(()), dma(()),
+            pltpu.VMEM((SET_ROWS, SET_ROWS), F32),
+            dma((4,)), dma((16,)), dma((4,)), dma(()), dma(()), dma((4,)),
             dma((2,)), dma((2,)), dma((2,)), dma((2,)), dma((2,)), dma((2,)),
         ],
         compiler_params=pltpu.CompilerParams(
-            collective_id=0, has_side_effects=True, vmem_limit_bytes=48 * 1024 * 1024
+            collective_id=0, has_side_effects=True, vmem_limit_bytes=(53 * 1024 + 768) * 1024
         ),
         cost_estimate=pl.CostEstimate(flops=700_000_000, bytes_accessed=8_000_000, transcendentals=0),
-    )(matrix, left_basis, right_basis, right_block)
+    )(matrix, left_basis.T, right_basis.T, right_block)
 
 
 def solution(mesh):

time: 98.7 us -> 84.8 us (0.86)
  Pallas kernels: 90.8 us -> 81.4 us
  local copies, waits for them, and re-layouts: 7 us -> 2.61 us
    pallas_call x1, Pallas kernels: 90.8 us -> 81.4 us  [shards(): pl.pallas_call(kernel, out_shape=(jax.ShapeDtypeStruct((BLOCK, WIDTH), F3...]
    unnamed x9 -> x5, local copies, waits for them, and re-layouts: 7 us -> 2.61 us
where the time goes in v2:
time: 84.8 us; the launch traced here: 84.7 us
  Pallas kernels  81.4 us (96%)
  local copies, waits for them, and re-layouts  2.61 us (3%)
    pallas_call x1, Pallas kernels, shards(): pl.pallas_call(kernel, out_shape=(jax.ShapeDtypeStruct((BLOCK, WIDTH), F3...  81.4 us
    unnamed x5, local copies, waits for them, and re-layouts  2.61 us

profile of v2, /device:TPU:1, one launch (start us, length us, event | category | flops | bytes accessed | tf_op | source)
XLA Modules:
  0.0 84.7 jit_solution(1917810139446752848)
XLA Ops:
  0.6 0.0 copy-start
  0.6 0.7 copy-done
  1.4 81.4 %shard_map.67 = (f32[64,96]{1,0:T(8,128)S(1)}, f32[64,96]{1,0:T(8,128)S(1)}, f32[2,64,64]{2,1,0:T(8,128)S(1)}) custom-call(bf16[768,3072]{1,0:T(8,128)(2,1)} %matrix_hbm.1, f32[96,320]{1,0:T(8,128)} %bitcast.2, f32[96,320]{1,0:T(8,128)} %bitcast.3, f32[64,96]{1,0:T(8,128)S(1)} %copy-done), custom_call_target="tpu_custom_call" | custom-call | flops 700000000 | bytes 8000000 | tf_op jit(solution)/shard_map/pallas_call | solution.py:389
  82.8 0.6 copy.10
  83.4 0.6 copy.11
  84.0 0.6 copy.12
Async XLA Ops:
  0.6 0.8 copy-start

commit v3 on v2

--- a/solution.py
+++ b/solution.py
@@ -33,6 +33,22 @@
 
 def lanes_of(shape):
     return lax.broadcasted_iota(jnp.int32, shape, 1)
+
+
+def valid_lanes(shape, q):
+    return lax.rem(lanes_of(shape) + 32 * q, LANES) < WIDTH
+
+
+def pack(values, q):
+    moved = jnp.concatenate([pltpu.roll(values[48:64, :], 32 * (3 - k), 1) for k in range(3)], axis=0)
+    return jnp.where(valid_lanes((48, LANES), q), values[0:48, :], moved)
+
+
+def unpack(packed, q):
+    group = lax.rem(lanes_of((16, LANES)) + 32 * q, LANES)
+    back = [pltpu.roll(packed[16 * k : 16 * k + 16, :], 32 * (1 + k), 1) for k in range(3)]
+    last = jnp.where(group < 32, back[0], jnp.where(group < 64, back[1], back[2]))
+    return jnp.concatenate([packed, last], axis=0)
 
 
 def cholesky_and_inverse(gram):
@@ -140,7 +156,7 @@
     left_set[0:BLOCK, :] = jnp.zeros((BLOCK, LANES), F32)
     left_set[0:BLOCK, 0:WIDTH] = block_in[...]
     turned_block = pltpu.roll(left_set[0:BLOCK, :], right_shift, 1)
-    b_slots[row] = turned_block.astype(BF16)
+    b_slots[row] = pack(turned_block, q_right).astype(BF16)
     pl.semaphore_wait(barrier, ROWS + COLS - 2)
     plane, within = row // 8, lax.rem(row, 8)
 
@@ -232,7 +248,7 @@
     def joined(slots):
         chunks = []
         for group in range(2):
-            first, second, third, fourth = (slots(4 * group + k).astype(F32) for k in range(4))
+            first, second, third, fourth = (unpack(slots(4 * group + k).astype(F32), k) for k in range(4))
             chunks.append(jnp.where(lane16 < 96, first, second).astype(BF16))
             chunks.append(jnp.where(lane16 < 64, second, third).astype(BF16))
             chunks.append(jnp.where(lane16 < 32, third, fourth).astype(BF16))
@@ -240,7 +256,8 @@
 
     def pieces(values):
         first, second, third = (values[:, 128 * k : 128 * k + 128] for k in range(3))
-        return (first, jnp.where(lane16 < 64, second, first), jnp.where(lane16 < 64, third, second), third)
+        turned_pieces = (first, jnp.where(lane16 < 64, second, first), jnp.where(lane16 < 64, third, second), third)
+        return [pack(piece, k) for k, piece in enumerate(turned_pieces)]
 
     load_matrix.wait()
     for y in (0, 1, 3, 2):
@@ -262,12 +279,12 @@
     send_col(lambda o, peer: image_send.at[peer], lambda o: image_recv.at[o - 1], image_sem, send_sem.at[7])
     start_gram(1, right_set)
     wait_bytes(image_recv, image_sem)
-    valid_left = lax.rem(lane16 + 32 * q_left, LANES) < WIDTH
-    valid_right = lax.rem(lane16 + 32 * q_right, LANES) < WIDTH
+    valid_left = valid_lanes((BLOCK, LANES), q_left)
+    valid_right = valid_lanes((BLOCK, LANES), q_right)
     image = image_send[col]
     for o in range(COLS - 1):
         image = image + image_recv[o]
-    image = jnp.where(valid_left, image, 0.0)
+    image = jnp.where(valid_left, unpack(image, q_left), 0.0)
 
     def sums_rs_send(side, values, basis):
         for i in range(3):
@@ -317,7 +334,7 @@
     sums_wait(0)
     gram_rs_send(1)
     left_new, left_upper = finish(0, image, left_set)
-    u_slots[col] = left_new.astype(BF16)
+    u_slots[col] = pack(left_new, q_left).astype(BF16)
     send_col(lambda o, peer: u_slots.at[col], lambda o: u_slots.at[col], u_sem, send_sem.at[14])
     gram_ar_send(1)
     left_out[...] = pltpu.roll(left_new, left_back, 1)[:, 0:WIDTH]
@@ -353,12 +370,12 @@
 
             lax.fori_loop(0, 8, send_piece_far, 0)
     co_recv[within] = co_send[row]
-    coimage = jnp.zeros((BLOCK, LANES), F32)
+    coimage = jnp.zeros((48, LANES), F32)
     for y in (0, 1, 3, 2):
         wait_bytes(co_recv.at[pl.ds(8 * y, 7 if y == 0 else 8)], co_sem.at[y])
         for w in range(8):
             coimage = coimage + co_recv[8 * y + w].astype(F32)
-    coimage = jnp.where(valid_right, coimage, 0.0)
+    coimage = jnp.where(valid_right, unpack(coimage, q_right), 0.0)
     sums_rs_send(1, coimage, right_set)
     sums_ar_send(1)
     gram_ag_send(1)
@@ -403,15 +420,15 @@
             pltpu.VMEM((LANES, SET_ROWS), F32),
             pltpu.VMEM((SET_ROWS, LANES), F32),
             pltpu.VMEM((SET_ROWS, LANES), F32),
-            pltpu.VMEM((ROWS, BLOCK, LANES), BF16),
+            pltpu.VMEM((ROWS, 48, LANES), BF16),
             pltpu.VMEM((BLOCK, 768), BF16),
             pltpu.VMEM((BLOCK, 768), F32),
-            pltpu.VMEM((COLS, BLOCK, LANES), F32),
-            pltpu.VMEM((COLS - 1, BLOCK, LANES), F32),
-            pltpu.VMEM((COLS, BLOCK, LANES), BF16),
+            pltpu.VMEM((COLS, 48, LANES), F32),
+            pltpu.VMEM((COLS - 1, 48, LANES), F32),
+            pltpu.VMEM((COLS, 48, LANES), BF16),
             pltpu.VMEM((BLOCK, 768), BF16),
-            pltpu.VMEM((ROWS, BLOCK, LANES), BF16),
-            pltpu.VMEM((ROWS, BLOCK, LANES), BF16),
+            pltpu.VMEM((ROWS, 48, LANES), BF16),
+            pltpu.VMEM((ROWS, 48, LANES), BF16),
             pltpu.VMEM((2, 256, LANES), F32),
             pltpu.VMEM((2, ROWS - 1, 8, LANES), F32),
             pltpu.VMEM((2, COLS, 8, LANES), F32),

time: 84.8 us -> 80.2 us (0.946)
  Pallas kernels: 81.4 us -> 76.8 us
    pallas_call x1, Pallas kernels: 81.4 us -> 76.8 us  [shards(): pl.pallas_call(kernel, out_shape=(jax.ShapeDtypeStruct((BLOCK, WIDTH), F3...]
where the time goes in v3:
time: 80.2 us; the launch traced here: 80.1 us
  Pallas kernels  76.8 us (96%)
  local copies, waits for them, and re-layouts  2.61 us (3%)
    pallas_call x1, Pallas kernels, shards(): pl.pallas_call(kernel, out_shape=(jax.ShapeDtypeStruct((BLOCK, WIDTH), F3...  76.8 us
    unnamed x5, local copies, waits for them, and re-layouts  2.61 us

profile of v3, /device:TPU:1, one launch (start us, length us, event | category | flops | bytes accessed | tf_op | source)
XLA Modules:
  0.0 80.1 jit_solution(826292423681233886)
XLA Ops:
  0.6 0.0 copy-start
  0.6 0.7 copy-done
  1.4 76.8 %shard_map.67 = (f32[64,96]{1,0:T(8,128)S(1)}, f32[64,96]{1,0:T(8,128)S(1)}, f32[2,64,64]{2,1,0:T(8,128)S(1)}) custom-call(bf16[768,3072]{1,0:T(8,128)(2,1)} %matrix_hbm.1, f32[96,320]{1,0:T(8,128)} %bitcast.2, f32[96,320]{1,0:T(8,128)} %bitcast.3, f32[64,96]{1,0:T(8,128)S(1)} %copy-done), custom_call_target="tpu_custom_call" | custom-call | flops 700000000 | bytes 8000000 | tf_op jit(solution)/shard_map/pallas_call | solution.py:406
  78.2 0.6 copy.10
  78.9 0.6 copy.11
  79.5 0.6 copy.12
Async XLA Ops:
  0.6 0.8 copy-start

commit v4 on v3

--- a/solution.py
+++ b/solution.py
@@ -85,10 +85,10 @@
     matrix, left_in, right_in, block_in,
     turned, left_set, right_set,
     b_slots, b_all, image_sum, image_send, image_recv,
-    u_slots, u_all, co_send, co_recv,
+    u_slots, u_all, pair_send, pair_recv, co_send, co_recv,
     p_local, p_rs, p_ar, p_all,
     g_local, g_rs, g_ar, g_all, weights,
-    load_sem, send_sem, b_sem, image_sem, u_sem, co_sem,
+    load_sem, send_sem, b_sem, pass_sem, image_sem, u_sem, pair_sem, co_sem,
     p_rs_sem, p_ar_sem, p_ag_sem, g_rs_sem, g_ar_sem, g_ag_sem,
 ):
     col = lax.axis_index("col")
@@ -156,33 +156,32 @@
     left_set[0:BLOCK, :] = jnp.zeros((BLOCK, LANES), F32)
     left_set[0:BLOCK, 0:WIDTH] = block_in[...]
     turned_block = pltpu.roll(left_set[0:BLOCK, :], right_shift, 1)
-    b_slots[row] = pack(turned_block, q_right).astype(BF16)
+    plane, across, core = row // 8, lax.rem(row, 8) // 2, lax.rem(row, 2)
+    sibling = row + 1 - 2 * core
+    own_slot = 8 * plane + 4 * core + across
+    b_slots[own_slot] = pack(turned_block, q_right).astype(BF16)
     pl.semaphore_wait(barrier, ROWS + COLS - 2)
-    plane, within = row // 8, lax.rem(row, 8)
-
-    def own_plane_peer(w):
-        return plane * 8 + lax.rem(within + w, 8)
-
-    def other_plane_peer(y, w):
-        return lax.rem(plane + y, 4) * 8 + lax.rem(within + w, 8)
-
-    def send_block(peer, y):
-        pltpu.make_async_remote_copy(
-            src_ref=b_slots.at[row], dst_ref=b_slots.at[row], send_sem=send_sem.at[0], recv_sem=b_sem.at[y],
-            device_id=(col, peer), device_id_type=MESH,
-        ).start()
-
-    def send_block_near(w, carry):
-        send_block(own_plane_peer(w), 0)
-        return carry
-
-    lax.fori_loop(1, 8, send_block_near, 0)
-    for y in (1, 3, 2):
-        def send_block_far(w, carry, y=y):
-            send_block(other_plane_peer(y, w), y)
+
+    def chip_peer(y, x):
+        return 8 * lax.rem(plane + y, 4) + 2 * x + core
+
+    def to_plane(y, send):
+        def near(w, carry):
+            x = lax.rem(across + w, 4)
+            send(chip_peer(y, x), x)
             return carry
 
-        lax.fori_loop(0, 8, send_block_far, 0)
+        lax.fori_loop(1 if y == 0 else 0, 4, near, 0)
+
+    for y in (0, 1, 3, 2):
+
+        def send_block(peer, x, y=y):
+            pltpu.make_async_remote_copy(
+                src_ref=b_slots.at[own_slot], dst_ref=b_slots.at[own_slot], send_sem=send_sem.at[0], recv_sem=b_sem.at[y],
+                device_id=(col, peer), device_id_type=MESH,
+            ).start()
+
+        to_plane(y, send_block)
 
     def turn(basis, q, out):
         for k in range(3):
@@ -260,12 +259,18 @@
         return [pack(piece, k) for k, piece in enumerate(turned_pieces)]
 
     load_matrix.wait()
-    for y in (0, 1, 3, 2):
-        wait_bytes(b_slots.at[pl.ds(0, 7 if y == 0 else 8)], b_sem.at[y])
+    def pass_to_sibling(y):
+        wait_bytes(b_slots.at[pl.ds(0, 3 if y == 0 else 4)], b_sem.at[y])
+        own = b_slots.at[pl.ds(8 * lax.rem(plane + (4 - y), 4) + 4 * core, 4)]
+        pltpu.make_async_remote_copy(
+            src_ref=own, dst_ref=own, send_sem=send_sem.at[16], recv_sem=pass_sem.at[y],
+            device_id=(col, sibling), device_id_type=MESH,
+        ).start()
+
+    def multiply(y):
+        wait_bytes(b_slots.at[pl.ds(0, 4)], pass_sem.at[y])
         source = lax.rem(plane + (4 - y), 4)
-        b_all[...] = joined(lambda k: b_slots[8 * source + k])
-        if y == 2:
-            gram_rs_send(0)
+        b_all[...] = joined(lambda k: b_slots[8 * source + 4 * (k % 2) + k // 2])
         part = lax.dot_general(
             b_all[...], matrix[:, pl.ds(pl.multiple_of(768 * source, 768), 768)], (((1,), (1,)), ((), ())), preferred_element_type=F32
         )
@@ -273,10 +278,20 @@
             image_sum[...] = part
         else:
             image_sum[...] += part
+
+    pass_to_sibling(0)
+    pass_to_sibling(1)
+    multiply(0)
+    pass_to_sibling(3)
+    multiply(1)
+    pass_to_sibling(2)
+    multiply(3)
+    multiply(2)
     for half in range(2):
         for k, piece in enumerate(pieces(image_sum[:, 384 * half : 384 * half + 384])):
             image_send[4 * half + k] = piece
     send_col(lambda o, peer: image_send.at[peer], lambda o: image_recv.at[o - 1], image_sem, send_sem.at[7])
+    gram_rs_send(0)
     start_gram(1, right_set)
     wait_bytes(image_recv, image_sem)
     valid_left = valid_lanes((BLOCK, LANES), q_left)
@@ -332,49 +347,57 @@
     sums_ag_send(0)
     gram_wait(0)
     sums_wait(0)
-    gram_rs_send(1)
     left_new, left_upper = finish(0, image, left_set)
     u_slots[col] = pack(left_new, q_left).astype(BF16)
     send_col(lambda o, peer: u_slots.at[col], lambda o: u_slots.at[col], u_sem, send_sem.at[14])
-    gram_ar_send(1)
+    gram_rs_send(1)
     left_out[...] = pltpu.roll(left_new, left_back, 1)[:, 0:WIDTH]
     write_factor(0, left_upper)
 
     wait_bytes(u_slots.at[pl.ds(0, COLS - 1)], u_sem)
     u_all[...] = joined(lambda k: u_slots[k])
 
-    def send_piece(peer, y):
-        pltpu.make_async_remote_copy(
-            src_ref=co_send.at[peer], dst_ref=co_recv.at[8 * y + within], send_sem=send_sem.at[15], recv_sem=co_sem.at[y],
-            device_id=(col, peer), device_id_type=MESH,
-        ).start()
-
-    for y in (2, 1, 3, 0):
+    def multiply_back(y):
         target = lax.rem(plane + y, 4)
         part = lax.dot_general(
             u_all[...], matrix[:, pl.ds(pl.multiple_of(768 * target, 768), 768)], (((1,), (0,)), ((), ())), preferred_element_type=F32
         )
         for half in range(2):
             for k, piece in enumerate(pieces(part[:, 384 * half : 384 * half + 384])):
-                co_send[8 * target + 4 * half + k] = piece.astype(BF16)
-        if y == 0:
-            def send_piece_near(w, carry):
-                send_piece(own_plane_peer(w), 0)
-                return carry
-
-            lax.fori_loop(1, 8, send_piece_near, 0)
-        else:
-            def send_piece_far(w, carry, y=y):
-                send_piece(other_plane_peer(y, w), y)
-                return carry
-
-            lax.fori_loop(0, 8, send_piece_far, 0)
-    co_recv[within] = co_send[row]
+                pair_send[y, k % 2, 2 * half + k // 2] = piece
+        pltpu.make_async_remote_copy(
+            src_ref=pair_send.at[y, 1 - core], dst_ref=pair_recv.at[y], send_sem=send_sem.at[17], recv_sem=pair_sem.at[y],
+            device_id=(col, sibling), device_id_type=MESH,
+        ).start()
+
+    def send_pieces(y):
+        wait_bytes(pair_recv.at[y], pair_sem.at[y])
+        for x in range(4):
+            co_send[y, x] = (pair_send[y, core, x] + pair_recv[y, x]).astype(BF16)
+
+        def send_piece(peer, x):
+            pltpu.make_async_remote_copy(
+                src_ref=co_send.at[y, x], dst_ref=co_recv.at[y, across], send_sem=send_sem.at[15], recv_sem=co_sem.at[y],
+                device_id=(col, peer), device_id_type=MESH,
+            ).start()
+
+        to_plane(y, send_piece)
+
+    multiply_back(2)
+    multiply_back(1)
+    send_pieces(2)
+    multiply_back(3)
+    send_pieces(1)
+    multiply_back(0)
+    send_pieces(3)
+    send_pieces(0)
+    co_recv[0, across] = co_send[0, across]
+    gram_ar_send(1)
     coimage = jnp.zeros((48, LANES), F32)
     for y in (0, 1, 3, 2):
-        wait_bytes(co_recv.at[pl.ds(8 * y, 7 if y == 0 else 8)], co_sem.at[y])
-        for w in range(8):
-            coimage = coimage + co_recv[8 * y + w].astype(F32)
+        wait_bytes(co_recv.at[y, pl.ds(0, 3 if y == 0 else 4)], co_sem.at[y])
+        for x in range(4):
+            coimage = coimage + co_recv[y, x].astype(F32)
     coimage = jnp.where(valid_right, unpack(coimage, q_right), 0.0)
     sums_rs_send(1, coimage, right_set)
     sums_ar_send(1)
@@ -386,10 +409,13 @@
     right_out[...] = pltpu.roll(right_new, right_back, 1)[:, 0:WIDTH]
     write_factor(1, right_upper)
 
-    wait_bytes(b_slots.at[pl.ds(0, ROWS - 1)], send_sem.at[0])
+    wait_bytes(b_slots.at[pl.ds(0, 15)], send_sem.at[0])
+    wait_bytes(b_slots.at[pl.ds(0, 16)], send_sem.at[16])
     wait_bytes(image_recv, send_sem.at[7])
     wait_bytes(u_slots.at[pl.ds(0, COLS - 1)], send_sem.at[14])
-    wait_bytes(co_recv.at[pl.ds(0, ROWS - 1)], send_sem.at[15])
+    for y in range(4):
+        wait_bytes(co_recv.at[y, pl.ds(0, 3 if y == 0 else 4)], send_sem.at[15])
+        wait_bytes(pair_recv.at[y], send_sem.at[17])
     for side in range(2):
         wait_bytes(g_rs.at[side], send_sem.at[1 + side])
         wait_bytes(g_ar.at[side, pl.ds(0, COLS - 1)], send_sem.at[3 + side])
@@ -427,8 +453,10 @@
             pltpu.VMEM((COLS - 1, 48, LANES), F32),
             pltpu.VMEM((COLS, 48, LANES), BF16),
             pltpu.VMEM((BLOCK, 768), BF16),
-            pltpu.VMEM((ROWS, 48, LANES), BF16),
-            pltpu.VMEM((ROWS, 48, LANES), BF16),
+            pltpu.VMEM((4, 2, 4, 48, LANES), F32),
+            pltpu.VMEM((4, 4, 48, LANES), F32),
+            pltpu.VMEM((4, 4, 48, LANES), BF16),
+            pltpu.VMEM((4, 4, 48, LANES), BF16),
             pltpu.VMEM((2, 256, LANES), F32),
             pltpu.VMEM((2, ROWS - 1, 8, LANES), F32),
             pltpu.VMEM((2, COLS, 8, LANES), F32),
@@ -438,7 +466,7 @@
             pltpu.VMEM((2, COLS, 24, LANES), F32),
             pltpu.VMEM((2, ROWS, 24, LANES), F32),
             pltpu.VMEM((SET_ROWS, SET_ROWS), F32),
-            dma((4,)), dma((16,)), dma((4,)), dma(()), dma(()), dma((4,)),
+            dma((4,)), dma((18,)), dma((4,)), dma((4,)), dma(()), dma(()), dma((4,)), dma((4,)),
             dma((2,)), dma((2,)), dma((2,)), dma((2,)), dma((2,)), dma((2,)),
         ],
         compiler_params=pltpu.CompilerParams(

time: 80.2 us -> 79.3 us (0.989)
  Pallas kernels: 76.8 us -> 75.9 us
    pallas_call x1, Pallas kernels: 76.8 us -> 75.9 us  [shards(): pl.pallas_call(kernel, out_shape=(jax.ShapeDtypeStruct((BLOCK, WIDTH), F3...]
where the time goes in v4:
time: 79.3 us; the launch traced here: 79.1 us
  Pallas kernels  75.9 us (96%)
  local copies, waits for them, and re-layouts  2.61 us (3%)
    pallas_call x1, Pallas kernels, shards(): pl.pallas_call(kernel, out_shape=(jax.ShapeDtypeStruct((BLOCK, WIDTH), F3...  75.9 us
    unnamed x5, local copies, waits for them, and re-layouts  2.61 us

profile of v4, /device:TPU:1, one launch (start us, length us, event | category | flops | bytes accessed | tf_op | source)
XLA Modules:
  0.0 79.1 jit_solution(7423676374547967568)
XLA Ops:
  0.6 0.0 copy-start
  0.6 0.7 copy-done
  1.4 75.9 %shard_map.67 = (f32[64,96]{1,0:T(8,128)S(1)}, f32[64,96]{1,0:T(8,128)S(1)}, f32[2,64,64]{2,1,0:T(8,128)S(1)}) custom-call(bf16[768,3072]{1,0:T(8,128)(2,1)} %matrix_hbm.1, f32[96,320]{1,0:T(8,128)} %bitcast.2, f32[96,320]{1,0:T(8,128)} %bitcast.3, f32[64,96]{1,0:T(8,128)S(1)} %copy-done), custom_call_target="tpu_custom_call" | custom-call | flops 700000000 | bytes 8000000 | tf_op jit(solution)/shard_map/pallas_call | solution.py:432
  77.3 0.6 copy.10
  77.9 0.6 copy.11
  78.5 0.6 copy.12
Async XLA Ops:
  0.6 0.8 copy-start

commit v5 on v4

--- a/solution.py
+++ b/solution.py
@@ -81,7 +81,7 @@
 
 def kernel(
     matrix_hbm, left_hbm, right_hbm, block_hbm,
-    left_out, right_out, factors_out,
+    found_out,
     matrix, left_in, right_in, block_in,
     turned, left_set, right_set,
     b_slots, b_all, image_sum, image_send, image_recv,
@@ -338,7 +338,7 @@
         return new_block, upper
 
     def write_factor(side, upper):
-        factors_out[side] = jnp.transpose(upper)[0:BLOCK, :]
+        found_out[128 + 64 * side : 192 + 64 * side, 0:BLOCK] = jnp.transpose(upper)[0:BLOCK, :]
 
     sums_rs_send(0, image, left_set)
     gram_ar_send(0)
@@ -351,7 +351,7 @@
     u_slots[col] = pack(left_new, q_left).astype(BF16)
     send_col(lambda o, peer: u_slots.at[col], lambda o: u_slots.at[col], u_sem, send_sem.at[14])
     gram_rs_send(1)
-    left_out[...] = pltpu.roll(left_new, left_back, 1)[:, 0:WIDTH]
+    found_out[0:64, :] = pltpu.roll(left_new, left_back, 1)
     write_factor(0, left_upper)
 
     wait_bytes(u_slots.at[pl.ds(0, COLS - 1)], u_sem)
@@ -406,7 +406,7 @@
     gram_wait(1)
     sums_wait(1)
     right_new, right_upper = finish(1, coimage, right_set)
-    right_out[...] = pltpu.roll(right_new, right_back, 1)[:, 0:WIDTH]
+    found_out[64:128, :] = pltpu.roll(right_new, right_back, 1)
     write_factor(1, right_upper)
 
     wait_bytes(b_slots.at[pl.ds(0, 15)], send_sem.at[0])
@@ -429,15 +429,11 @@
     in_hbm = pl.BlockSpec(memory_space=pltpu.HBM)
     in_vmem = pl.BlockSpec(memory_space=pltpu.VMEM)
     dma = pltpu.SemaphoreType.DMA
-    return pl.pallas_call(
+    found = pl.pallas_call(
         kernel,
-        out_shape=(
-            jax.ShapeDtypeStruct((BLOCK, WIDTH), F32),
-            jax.ShapeDtypeStruct((BLOCK, WIDTH), F32),
-            jax.ShapeDtypeStruct((2, BLOCK, BLOCK), F32),
-        ),
+        out_shape=jax.ShapeDtypeStruct((4 * BLOCK, LANES), F32),
         in_specs=[in_hbm] * 4,
-        out_specs=(in_vmem, in_vmem, in_vmem),
+        out_specs=in_vmem,
         scratch_shapes=[
             pltpu.VMEM((768, 3072), BF16),
             pltpu.VMEM((WIDTH, PRIOR_ROWS), F32),
@@ -474,6 +470,8 @@
         ),
         cost_estimate=pl.CostEstimate(flops=700_000_000, bytes_accessed=8_000_000, transcendentals=0),
     )(matrix, left_basis.T, right_basis.T, right_block)
+    factors = found[128:256, 0:BLOCK].reshape(2, BLOCK, BLOCK)
+    return found[0:64, 0:WIDTH], found[64:128, 0:WIDTH], factors
 
 
 def solution(mesh):

time: 79.3 us -> 78.7 us (level)
    unnamed x5 -> x2, local copies, waits for them, and re-layouts: 2.61 us -> 0.75 us
    slice x0 -> x2, local copies, waits for them, and re-layouts: none -> 1.26 us  [the longest x1 0.63 us: shards(): factors = found[128:256, 0:BLOCK].reshape(2, BLOCK, BLOCK)]
where the time goes in v5:
time: 78.7 us; the launch traced here: 78.5 us
  Pallas kernels  75.9 us (96%)
  local copies, waits for them, and re-layouts  2.02 us (3%)
    pallas_call x1, Pallas kernels, shards(): pl.pallas_call(kernel, out_shape=jax.ShapeDtypeStruct((4 * BLOCK, LANES),...  75.9 us

profile of v5, /device:TPU:1, one launch (start us, length us, event | category | flops | bytes accessed | tf_op | source)
XLA Modules:
  0.0 78.5 jit_solution(265657038847815424)
XLA Ops:
  0.6 0.0 copy-start
  0.6 0.7 copy-done
  1.4 75.9 %shard_map.67 = f32[256,128]{1,0:T(8,128)S(1)} custom-call(bf16[768,3072]{1,0:T(8,128)(2,1)} %matrix_hbm.1, f32[96,320]{1,0:T(8,128)} %bitcast.3, f32[96,320]{1,0:T(8,128)} %bitcast.4, f32[64,96]{1,0:T(8,128)S(1)} %copy-done), custom_call_target="tpu_custom_call" | custom-call | flops 700000000 | bytes 8000000 | tf_op jit(solution)/shard_map/pallas_call | solution.py:432
  77.3 0.6 fusion
  77.9 0.6 slice.11
Async XLA Ops:
  0.6 0.8 copy-start

commit v6 on v5

--- a/solution.py
+++ b/solution.py
@@ -133,7 +133,7 @@
             ).start()
             return carry
 
-        lax.fori_loop(0, ROWS - 1, body, 0)
+        lax.fori_loop(0, ROWS - 1, body, 0, unroll=True)
 
     def send_col(source, target, sem, send):
         def body(k, carry):
@@ -145,7 +145,7 @@
             ).start()
             return carry
 
-        lax.fori_loop(0, COLS - 1, body, 0)
+        lax.fori_loop(0, COLS - 1, body, 0, unroll=True)
 
     right_shift = lax.rem(96 * q_right, LANES)
     right_back = lax.rem(32 * q_right, LANES)
@@ -171,7 +171,7 @@
             send(chip_peer(y, x), x)
             return carry
 
-        lax.fori_loop(1 if y == 0 else 0, 4, near, 0)
+        lax.fori_loop(1 if y == 0 else 0, 4, near, 0, unroll=True)
 
     for y in (0, 1, 3, 2):
 

time: 78.7 us -> 78 us (level)
  no operation moved by 1% of the time
where the time goes in v6:
time: 78 us; the launch traced here: 77.9 us
  Pallas kernels  75.2 us (96%)
  local copies, waits for them, and re-layouts  2.02 us (3%)
    pallas_call x1, Pallas kernels, shards(): pl.pallas_call(kernel, out_shape=jax.ShapeDtypeStruct((4 * BLOCK, LANES),...  75.2 us

profile of v6, /device:TPU:1, one launch (start us, length us, event | category | flops | bytes accessed | tf_op | source)
XLA Modules:
  0.0 77.9 jit_solution(6440579584229122740)
XLA Ops:
  0.6 0.0 copy-start
  0.6 0.7 copy-done
  1.4 75.2 %shard_map.67 = f32[256,128]{1,0:T(8,128)S(1)} custom-call(bf16[768,3072]{1,0:T(8,128)(2,1)} %matrix_hbm.1, f32[96,320]{1,0:T(8,128)} %bitcast.3, f32[96,320]{1,0:T(8,128)} %bitcast.4, f32[64,96]{1,0:T(8,128)S(1)} %copy-done), custom_call_target="tpu_custom_call" | custom-call | flops 700000000 | bytes 8000000 | tf_op jit(solution)/shard_map/pallas_call | solution.py:432
  76.6 0.6 fusion
  77.2 0.6 slice.11
Async XLA Ops:
  0.6 0.8 copy-start
